TPU v7x, 32 devices: a whole 2x2x4 slice. The times are simulated.
32 devices in a mesh: polar: 4 (over y, x), azimuth: 8 (over z, core).
Axes of the slice: x: 2, y: 2, z: 4, core: 2. Of those that a mesh axis runs over, the one named last changes fastest.
Arguments:
- state: float32 [2, 32, 72, 1440], P(None, 'polar', None, 'azimuth'), may hold values from -6 to 6
- kernels: float32 [9, 3, 9, 72], replicated, may hold values from -1.25 to 1.25
- kernel_index: int32 [16], replicated, may hold values from 0 to 8
- w_mix: float32 [72, 641], replicated, may hold values from -0.75 to 0.75
- w_in: float32 [641, 1282], replicated, may hold values from -0.25 to 0.25
- b_in: float32 [1282], replicated, may hold values from -4 to 4
- w_out: float32 [1282, 641], replicated, may hold values from -0.15625 to 0.15625
Outputs:
- encoded: float32 [2, 16, 1440, 641], P(None, 'polar', 'azimuth')
All inputs are finite; a program needn't handle non-finite values.
Results may differ from a plain program's by a relative error of at most 0.000065.
Values sent between devices are 32-bit elements; how exact they have to be, the bound alone decides.
A program may use at most 64 MiB of HBM per device.

v0:
```python
import functools

import jax
import jax.numpy as jnp
from jax import lax
from jax.experimental import pallas as pl
from jax.experimental.pallas import tpu as pltpu
from jax.sharding import PartitionSpec as P

TAPS = 9
SPACING = 90


def shifted(array, axis, by):
    peers = lax.axis_size(axis)
    pairs = [(i, i + by) for i in range(peers) if 0 <= i + by < peers]
    return lax.ppermute(array, axis, pairs)


def row_taps(kernels, kernel_index, out_lat, tap_pos, channel, valid):
    fields = kernels.shape[3]
    total_out = kernel_index.shape[0]
    pick = (out_lat[:, None] == jnp.arange(total_out, dtype=jnp.int32)[None, :]).astype(jnp.int32)
    kernel_of = jnp.sum(pick * kernel_index[None, :], axis=1)
    one_kernel = (
        kernel_of[:, None] == jnp.arange(kernels.shape[0], dtype=jnp.int32)[None, :]
    ).astype(jnp.float32)
    one_tap = (tap_pos[:, None] == jnp.arange(3, dtype=jnp.int32)[None, :]).astype(jnp.float32)
    one_field = (channel[:, None] == jnp.arange(fields, dtype=jnp.int32)[None, :]).astype(
        jnp.float32
    )
    chosen = jnp.einsum(
        "rk,ra,rc,katc->rt",
        one_kernel,
        one_tap,
        one_field,
        kernels,
        precision=lax.Precision.HIGHEST,
        preferred_element_type=jnp.float32,
    )
    return chosen * valid[:, None]


def correlate(cycle, weights):
    half = TAPS // 2
    total = jnp.zeros(cycle.shape, jnp.float32)
    for tap in range(TAPS):
        total = total + weights[:, tap : tap + 1] * jnp.roll(cycle, -(tap - half) * SPACING, axis=1)
    return total


def finish(summed, w_mix, w_in, b_in, w_out):
    lat_half, fields, lon_dev = summed.shape
    mixed = jnp.einsum(
        "ocl,ce->ole",
        summed,
        w_mix,
        precision=lax.Precision.HIGHEST,
        preferred_element_type=jnp.float32,
    ).reshape(lat_half * lon_dev, -1)
    pre = (
        jnp.dot(mixed, w_in, precision=lax.Precision.HIGHEST, preferred_element_type=jnp.float32)
        + b_in
    )
    hidden = jax.nn.gelu(pre, approximate=False)
    out = mixed + jnp.dot(
        hidden, w_out, precision=lax.Precision.HIGHEST, preferred_element_type=jnp.float32
    )
    return out.reshape(lat_half, lon_dev, -1)


def per_device(state, kernels, kernel_index, w_mix, w_in, b_in, w_out):
    members, lat_dev, fields, lon_dev = state.shape
    lat_half = lat_dev // 2
    azim = lax.axis_index("azimuth")
    band = lax.axis_index("polar")
    total_out = kernel_index.shape[0]
    results = []
    for member in range(members):
        block = state[member]
        flat = block.reshape(lat_dev * fields, lon_dev)
        cycle = lax.all_to_all(flat, "azimuth", split_axis=0, concat_axis=1, tiled=True)
        rows_here = cycle.shape[0]
        index = azim * rows_here + jnp.arange(rows_here, dtype=jnp.int32)
        glob = band * lat_dev + index // fields
        channel = index % fields
        parity = glob % 2
        first_w = row_taps(
            kernels,
            kernel_index,
            glob // 2,
            1 + parity,
            channel,
            jnp.ones((rows_here,), jnp.float32),
        )
        second_out = (glob + 1) // 2
        second_ok = ((parity == 1) & (second_out < total_out)).astype(jnp.float32)
        second_w = row_taps(
            kernels, kernel_index, second_out, jnp.zeros_like(glob), channel, second_ok
        )
        planes = jnp.stack([correlate(cycle, first_w), correlate(cycle, second_w)])
        back = lax.all_to_all(planes, "azimuth", split_axis=2, concat_axis=1, tiled=True)
        back = back.reshape(2, lat_half, 2, fields, lon_dev)
        near = back[0, :, 0] + back[0, :, 1]
        upper = back[1, :, 1]
        edge = shifted(upper[-1], "polar", 1)
        summed = near + jnp.concatenate([edge[None], upper[:-1]], axis=0)
        results.append(finish(summed, w_mix, w_in, b_in, w_out))
    return jnp.stack(results)


LANES = 128
SUB = 8
GROUP = 4
WIDE = 256
EARLY = 3
MESH = pl.DeviceIdType.MESH


def halves(x):
    top = x.astype(jnp.bfloat16).astype(jnp.float32)
    return top, x - top


def room_of(lon_dev):
    return -(-(lon_dev // 2 * GROUP) // 16) * 16


def mlp_rows(fields, extra, left16, first, rest, second, held):
    main = first.shape[1]
    at = 3 * fields + 3
    low_at = at + 2 * extra

    def act(weights):
        pre = jnp.dot(left16, weights, preferred_element_type=jnp.float32)
        return pre * 0.5 * (1.0 + lax.erf(pre * (0.5**0.5)))

    for c in range(main // WIDE):
        hidden = act(first[:, c * WIDE : (c + 1) * WIDE])
        top = hidden.astype(jnp.bfloat16)
        low = (hidden - top.astype(jnp.float32)).astype(jnp.bfloat16)
        held[:, c * WIDE : (c + 1) * WIDE] = top
        held[:, main + c * WIDE : main + (c + 1) * WIDE] = top
        held[:, 2 * main + c * WIDE : 2 * main + (c + 1) * WIDE] = low
    top, low = halves(act(rest[...]))
    lane = lax.broadcasted_iota(jnp.int32, top.shape, 1)
    mixed = jnp.where(
        lane < at,
        left16.astype(jnp.float32),
        jnp.where(lane < low_at, top, jnp.where(lane < low_at + extra, low, 0.0)),
    )
    held[:, 3 * main :] = mixed.astype(jnp.bfloat16)
    return lambda: jnp.dot(held[...], second[...], preferred_element_type=jnp.float32)


def exchange(
    bands,
    columns,
    early,
    idx_ref,
    kern,
    w_mix,
    b_in,
    st_hbm,
    w_in_hbm,
    w_out_hbm,
    left_out,
    first_out,
    rest_out,
    second_out,
    early_out,
    st,
    w_in,
    w_out,
    first,
    rest,
    second,
    left,
    rows_f32,
    held,
    result,
    peer,
    edge,
    blocks,
    taps,
    own,
    outgoing,
    incoming,
    load_sem,
    store_sem,
    result_sem,
    peer_send,
    peer_recv,
    edge_send,
    edge_recv,
    part_send,
    part_recv,
):
    members, lat_dev, fields, lon_dev = st.shape
    lat_half = lat_dev // 2
    tiles = fields // SUB
    embed, ffn = w_in.shape
    pieces = 2 * members
    az = lax.axis_index("azimuth")
    band = lax.axis_index("polar")
    core = lax.rem(az, 2)
    chip = az // 2
    chips = columns // 2
    mate = chip * 2 + 1 - core
    up = lax.rem(chip + 1, chips) * 2 + core
    down = lax.rem(chip + chips - 1, chips) * 2 + core
    next_band = lax.rem(band + 1, bands)
    last_band = lax.rem(band + bands - 1, bands)

    loads = [pltpu.make_async_copy(st_hbm.at[m], st.at[m], load_sem.at[m]) for m in range(members)]
    load_in = pltpu.make_async_copy(w_in_hbm, w_in, load_sem.at[members])
    load_out = pltpu.make_async_copy(w_out_hbm, w_out, load_sem.at[members + 1])
    for copy in loads:
        copy.start()

    barrier = pltpu.get_barrier_semaphore()
    for who in ((band, mate), (band, up), (band, down), (last_band, az), (last_band, mate)):
        pl.semaphore_signal(barrier, inc=1, device_id=who, device_id_type=MESH)
    pl.semaphore_wait(barrier, 5)

    def remote(src, dst, send, recv, who):
        return pltpu.make_async_remote_copy(
            src_ref=src, dst_ref=dst, send_sem=send, recv_sem=recv, device_id=who, device_id_type=MESH
        )

    peers = []
    edges = []
    for m in range(members):
        peers.append(remote(st_hbm.at[m], peer.at[m], peer_send.at[m], peer_recv.at[m], (band, mate)))
        edges.append(
            [
                remote(
                    st_hbm.at[m, lat_dev - 1],
                    edge.at[s, m],
                    edge_send.at[s, m],
                    edge_recv.at[s, m],
                    (next_band, who),
                )
                for s, who in enumerate((az, mate))
            ]
        )
    for m in range(members):
        for copy in edges[m]:
            copy.start()
        peers[m].start()
    load_in.start()
    load_out.start()

    half = TAPS // 2
    pad = half - 1
    for o in range(lat_half):
        k = idx_ref[band * lat_half + o]
        for a in range(3):
            columns_of = kern[k, :, a, :].T
            if o == 0 and a == 0:
                columns_of = columns_of * jnp.where(band > 0, 1.0, 0.0)
            for t in range(TAPS):
                taps[o * 3 + a, t + pad] = jnp.broadcast_to(columns_of[:, t : t + 1], (fields, LANES))
            for t in range(pad):
                taps[o * 3 + a, t] = jnp.zeros((fields, LANES), jnp.float32)
                taps[o * 3 + a, t + pad + TAPS] = jnp.zeros((fields, LANES), jnp.float32)

    spare = lon_dev - LANES

    def unpack(src, m, lat, to):
        x = src[:, :LANES]
        y = src[:, LANES:]
        y = jnp.concatenate([y, jnp.zeros((fields, LANES - spare), jnp.float32)], axis=1)
        lane = lax.broadcasted_iota(jnp.int32, x.shape, 1)
        blocks[m, lat, to] = x
        blocks[m, lat, to + 1] = pltpu.roll(jnp.where(lane < SPACING, y, x), LANES - SPACING, 1)

    turns = [q * SPACING % LANES for q in range(GROUP)]

    def pack(value, ref, at, rows):
        lane = lax.broadcasted_iota(jnp.int32, (SUB, LANES), 1)
        turned = [value[0]] + [pltpu.roll(value[q], turns[q], 1) for q in range(1, GROUP)]
        ref[at + (0, rows, slice(None))] = jnp.where(lane < turns[1], turned[0], turned[1])
        ref[at + (1, rows, slice(None))] = jnp.where(lane < turns[2], turned[1], turned[2])
        ref[at + (2, rows, slice(None))] = jnp.where(lane < turns[3], turned[2], turned[3])

    def correlate_member(m):
        def body(r, carry):
            rows = pl.ds(pl.multiple_of(r * SUB, SUB), SUB)
            total = [[[None] * lat_half for _ in range(2)] for _ in range(3)]
            for o in range(lat_half):
                for a in range(3):
                    x = [blocks[m, 2 * o + a, b, rows, :] for b in range(4)]
                    for target in range(3):
                        base = pad + half * target - 2 * core
                        w = {d: taps[o * 3 + a, base + d, rows, :] for d in range(-1, 4)}
                        for j in range(2):
                            term = w[-j] * x[0]
                            for b in range(1, 4):
                                term = term + w[b - j] * x[b]
                            old = total[target][j][o]
                            total[target][j][o] = term if old is None else old + term
            for j in range(2):
                pack(total[0][j], outgoing, (0, 2 * m + j), rows)
                pack(total[1][j], own, (2 * m + j,), rows)
                pack(total[2][j], outgoing, (1, 2 * m + j), rows)
            return carry

        lax.fori_loop(0, tiles, body, 0)

    def parts(k):
        return [
            remote(
                outgoing.at[way, k],
                incoming.at[way, k],
                part_send.at[way, k],
                part_recv.at[way, k],
                (band, who),
            )
            for way, who in enumerate((up, down))
        ]

    mine = 2 * core
    theirs = 2 - 2 * core
    for m in range(members):
        loads[m].wait()
        for lat in range(lat_dev):
            unpack(st.at[m, lat], m, lat + 1, mine)
        peers[m].wait()
        for lat in range(lat_dev):
            unpack(peer.at[m, lat], m, lat + 1, theirs)
        for copy in edges[m]:
            copy.wait()
        unpack(edge.at[0, m], m, 0, mine)
        unpack(edge.at[1, m], m, 0, theirs)
        correlate_member(m)
        for j in range(2):
            for copy in parts(2 * m + j):
                copy.start()

    main = ffn // WIDE * WIDE
    extra = ffn - main
    at = 3 * fields + 3
    mix_top, mix_low = halves(w_mix[...])
    stacked = jnp.concatenate([mix_top, mix_low], axis=0).astype(jnp.bfloat16)
    load_in.wait()

    def product(cols):
        in_top, in_low = halves(w_in[:, cols])
        big = jnp.dot(stacked, in_top.astype(jnp.bfloat16), preferred_element_type=jnp.float32)
        small = jnp.dot(
            mix_top.astype(jnp.bfloat16), in_low.astype(jnp.bfloat16), preferred_element_type=jnp.float32
        )
        whole = big[:fields] + (big[fields:] + small)
        top, low = halves(whole)
        bias, leave = halves(b_in[cols][None, :])
        bias_low, leave = halves(leave)
        width = whole.shape[1]
        return jnp.concatenate(
            [top, low, top, bias, bias_low, leave, jnp.zeros((WIDE - at, width), jnp.float32)], axis=0
        )

    for c in range(main // WIDE):
        cols = slice(c * WIDE, (c + 1) * WIDE)
        first[:, cols] = product(cols).astype(jnp.bfloat16)
    tail = product(slice(main, ffn))
    rest[...] = jnp.concatenate(
        [jnp.zeros((WIDE, at), jnp.float32)]
        + [tail] * 3
        + [jnp.zeros((WIDE, WIDE - at - 3 * extra), jnp.float32)],
        axis=1,
    ).astype(jnp.bfloat16)
    load_out.wait()
    for c in range(main // WIDE):
        top, low = halves(w_out[:, c * WIDE : (c + 1) * WIDE].T)
        base = c * WIDE
        second[base : base + WIDE, :] = top.astype(jnp.bfloat16)
        second[base + main : base + main + WIDE, :] = low.astype(jnp.bfloat16)
        second[base + 2 * main : base + 2 * main + WIDE, :] = top.astype(jnp.bfloat16)
    top, low = halves(w_out[:, main:].T)
    second[3 * main :, :] = jnp.concatenate(
        [mix_top, mix_low, mix_top, jnp.zeros((3, embed), jnp.float32), top, low, top]
        + [jnp.zeros((WIDE - at - 3 * extra, embed), jnp.float32)],
        axis=0,
    ).astype(jnp.bfloat16)
    stores = [
        pltpu.make_async_copy(src, dst, store_sem.at[i])
        for i, (src, dst) in enumerate(((first, first_out), (rest, rest_out), (second, second_out)))
    ]
    for copy in stores:
        copy.start()

    count = lon_dev // 2
    room = rows_f32.shape[1]
    for side in range(WIDE // LANES):
        rows_f32[side, count * GROUP :, :] = jnp.zeros((room - count * GROUP, LANES), jnp.float32)

    def finish_part(k):
        for copy in parts(k):
            copy.wait()
        v = [own[k, i] + incoming[0, k, i] + incoming[1, k, i] for i in range(GROUP - 1)]
        lane = lax.broadcasted_iota(jnp.int32, v[0].shape, 1)
        fields_of = [v[0]]
        for q in range(1, GROUP):
            both = v[q - 1] if q == GROUP - 1 else jnp.where(lane >= turns[q], v[q - 1], v[q])
            fields_of.append(pltpu.roll(both, LANES - turns[q], 1))
        for q in range(GROUP):
            top, low = halves(fields_of[q])
            flat = jnp.concatenate(
                [top, top, low, jnp.ones((3, LANES), jnp.float32)]
                + [jnp.zeros((WIDE - at, LANES), jnp.float32)],
                axis=0,
            )
            turned = flat.T[:count]
            for side in range(WIDE // LANES):
                rows_f32[side, pl.ds(q, count, stride=GROUP), :] = turned[
                    :, side * LANES : (side + 1) * LANES
                ]
        return jnp.concatenate([rows_f32[side] for side in range(WIDE // LANES)], axis=1).astype(
            jnp.bfloat16
        )

    def early_piece(k, carry):
        left[...] = finish_part(k)
        total = mlp_rows(fields, extra, left[...], first, rest, second, held)()
        result[...] = total[: count * GROUP].reshape(count, GROUP, embed)
        copy = pltpu.make_async_copy(result, early_out.at[k], result_sem)
        copy.start()
        copy.wait()
        return carry

    if early:
        lax.fori_loop(0, early, early_piece, 0)
    for k in range(early, pieces):
        left_out[k - early] = finish_part(k)
    for copy in stores:
        copy.wait()


def mlp(
    fields, extra, early, left_ref, first, rest, second_hbm, early_in, out, second, held, result, load_sem, move_sem, result_sem
):
    late = left_ref.shape[0]
    count = result.shape[0]
    embed = result.shape[2]
    load = pltpu.make_async_copy(second_hbm, second, load_sem)
    load.start()
    moves = [
        pltpu.make_async_copy(
            early_in.at[k], out.at[k // 2, pl.ds(k % 2 * count, count)], move_sem.at[k]
        )
        for k in range(early)
    ]
    for copy in moves:
        copy.start()
    for i in range(late):
        k = early + i
        finish = mlp_rows(fields, extra, left_ref[i], first, rest, second, held)
        if i == 0:
            load.wait()
        result[...] = finish()[: count * GROUP].reshape(count, GROUP, embed)
        copy = pltpu.make_async_copy(
            result, out.at[k // 2, pl.ds(k % 2 * count, count)], result_sem
        )
        copy.start()
        copy.wait()
    for copy in moves:
        copy.wait()


def per_device_fast(bands, columns, state, kernels, kernel_index, w_mix, w_in, b_in, w_out):
    members, lat_dev, fields, lon_dev = state.shape
    lat_half = lat_dev // 2
    pieces = 2 * members
    early = min(EARLY, pieces - 1)
    late = pieces - early
    count = lon_dev // 2
    embed, ffn = w_in.shape
    main = ffn // WIDE * WIDE
    depth = 3 * main + WIDE
    room = room_of(lon_dev)
    vmem = pl.BlockSpec(memory_space=pltpu.VMEM)
    hbm = pl.BlockSpec(memory_space=pl.ANY)
    f32 = jnp.float32
    half = jnp.bfloat16
    dma = pltpu.SemaphoreType.DMA
    packed = (pieces, GROUP - 1, fields, LANES)
    left, first, rest, second, ready = pl.pallas_call(
        functools.partial(exchange, bands, columns, early),
        out_shape=(
            jax.ShapeDtypeStruct((late, room, WIDE), half),
            jax.ShapeDtypeStruct((WIDE, main), half),
            jax.ShapeDtypeStruct((WIDE, WIDE), half),
            jax.ShapeDtypeStruct((depth, embed), half),
            jax.ShapeDtypeStruct((early, count, GROUP, embed), f32),
        ),
        in_specs=[pl.BlockSpec(memory_space=pltpu.SMEM)] + [vmem] * 3 + [hbm] * 3,
        out_specs=(vmem,) + (hbm,) * 4,
        scratch_shapes=[
            pltpu.VMEM(state.shape, f32),
            pltpu.VMEM(w_in.shape, f32),
            pltpu.VMEM(w_out.shape[::-1], f32),
            pltpu.VMEM((WIDE, main), half),
            pltpu.VMEM((WIDE, WIDE), half),
            pltpu.VMEM((depth, embed), half),
            pltpu.VMEM((room, WIDE), half),
            pltpu.VMEM((WIDE // LANES, room, LANES), f32),
            pltpu.VMEM((room, depth), half),
            pltpu.VMEM((count, GROUP, embed), f32),
            pltpu.VMEM(state.shape, f32),
            pltpu.VMEM((2, members, fields, lon_dev), f32),
            pltpu.VMEM((members, lat_dev + 1, 4, fields, LANES), f32),
            pltpu.VMEM((lat_half * 3, 2 * TAPS - 3, fields, LANES), f32),
            pltpu.VMEM(packed, f32),
            pltpu.VMEM((2,) + packed, f32),
            pltpu.VMEM((2,) + packed, f32),
            dma((members + 2,)),
            dma((3,)),
            dma(()),
            dma((members,)),
            dma((members,)),
            dma((2, members)),
            dma((2, members)),
            dma((2, pieces)),
            dma((2, pieces)),
        ],
        compiler_params=pltpu.CompilerParams(
            collective_id=0, has_side_effects=True, vmem_limit_bytes=60 * 2**20
        ),
        name="exchange",
    )(
        kernel_index,
        jnp.transpose(kernels, (0, 2, 1, 3)),
        w_mix,
        b_in,
        state,
        w_in,
        w_out.T,
    )
    out = pl.pallas_call(
        functools.partial(mlp, fields, ffn - main, early),
        out_shape=jax.ShapeDtypeStruct((members, lon_dev, lat_half, embed), f32),
        in_specs=[vmem] * 3 + [hbm] * 2,
        out_specs=hbm,
        scratch_shapes=[
            pltpu.VMEM((depth, embed), half),
            pltpu.VMEM((room, depth), half),
            pltpu.VMEM((count, GROUP, embed), f32),
            dma(()),
            dma((early,)),
            dma(()),
        ],
        compiler_params=pltpu.CompilerParams(vmem_limit_bytes=56 * 2**20),
        name="mlp",
    )(left, first, rest, second, ready)
    return jnp.transpose(out, (0, 2, 1, 3))


def fits(mesh, state, w_in):
    bands, columns = mesh.shape["polar"], mesh.shape["azimuth"]
    members, lat, fields, lon = state.shape
    main = w_in.shape[1] // WIDE * WIDE
    return (
        bands >= 2
        and columns % 2 == 0
        and columns >= 6
        and lon == 2 * SPACING * columns
        and lat == 2 * GROUP * bands
        and fields % SUB == 0
        and main > 0
        and 3 * fields + 3 + 3 * (w_in.shape[1] - main) <= WIDE
    )


def solution(mesh):
    placed = (P(None, "polar", None, "azimuth"), P(), P(), P(), P(), P(), P())

    def run(state, kernels, kernel_index, w_mix, w_in, b_in, w_out):
        body = per_device
        if fits(mesh, state, w_in):
            body = functools.partial(per_device_fast, mesh.shape["polar"], mesh.shape["azimuth"])
        return jax.shard_map(
            body,
            mesh=mesh,
            in_specs=placed,
            out_specs=P(None, "polar", "azimuth", None),
            check_vma=False,
        )(state, kernels, kernel_index, w_mix, w_in, b_in, w_out)

    return run
```

profile of v0, /device:TPU:0, one launch (start us, length us, event | category | flops | bytes accessed | tf_op | source)
XLA Modules:
  0.0 136.8 jit_solution(6242786701632785721)
XLA Ops:
  0.0 34.0 %exchange.1 = (bf16[1,368,256]{2,1,0:T(8,128)(2,1)}, bf16[256,1280]{1,0:T(8,128)(2,1)}, bf16[256,256]{1,0:T(8,128)(2,1)}, bf16[4096,641]{1,0:T(8,128)(2,1)}, f32[3,90,4,641]{3,2,1,0:T(4,128)}) custom-call(s32[16]{0:T(128)} %idx_ref.1, f32[9,9,3,72]{3,2,1,0:T(4,128)} %bitcast.4, f32[72,641]{1,0:T(8,128)} %w_mix.1, f32[1282]{0:T(1024)} %b_in.1, ...), custom_call_target="tpu_custom_call" | custom-call | tf_op jit(solution)/shard_map/exchange/pallas_call | solution.py:488
  34.0 102.8 %mlp.1 = f32[2,180,4,641]{3,2,1,0:T(4,128)} custom-call(bf16[1,368,256]{2,1,0:T(8,128)(2,1)} %get-tuple-element.10.left_ref, bf16[256,1280]{1,0:T(8,128)(2,1)} %get-tuple-element.11.first, bf16[256,256]{1,0:T(8,128)(2,1)} %get-tuple-element.12.rest, bf16[4096,641]{1,0:T(8,128)(2,1)} %get-tuple-element.13.second_hbm, f32[3,90,4,641]{3,2,1,0:T(4,128)} %get-tuple-element.14.early_in), custom_call_target="tpu_custom_call" | custom-call | tf_op jit(solution)/shard_map/mlp/pallas_call | solution.py:540
where the time goes:
time: 138 us; the launch traced here: 137 us
  Pallas kernels  137 us (99%)
    pallas_call x1, Pallas kernels, per_device_fast(): pl.pallas_call(functools.partial(mlp, fields, ffn - main, early), out_sha...  103 us
    pallas_call x1, Pallas kernels, per_device_fast(): pl.pallas_call(functools.partial(exchange, bands, columns, early), out_sh...  34 us

commit v1 on v0

--- a/solution.py
+++ b/solution.py
@@ -113,7 +113,6 @@
 SUB = 8
 GROUP = 4
 WIDE = 256
-EARLY = 3
 MESH = pl.DeviceIdType.MESH
 
 
@@ -156,7 +155,6 @@
 def exchange(
     bands,
     columns,
-    early,
     idx_ref,
     kern,
     w_mix,
@@ -164,10 +162,6 @@
     st_hbm,
     w_in_hbm,
     w_out_hbm,
-    left_out,
-    first_out,
-    rest_out,
-    second_out,
     early_out,
     st,
     w_in,
@@ -187,12 +181,13 @@
     outgoing,
     incoming,
     load_sem,
-    store_sem,
     result_sem,
     peer_send,
     peer_recv,
     edge_send,
     edge_recv,
+    relay_send,
+    relay_recv,
     part_send,
     part_recv,
 ):
@@ -219,9 +214,9 @@
         copy.start()
 
     barrier = pltpu.get_barrier_semaphore()
-    for who in ((band, mate), (band, up), (band, down), (last_band, az), (last_band, mate)):
+    for who in ((band, mate), (band, up), (band, down), (last_band, az)):
         pl.semaphore_signal(barrier, inc=1, device_id=who, device_id_type=MESH)
-    pl.semaphore_wait(barrier, 5)
+    pl.semaphore_wait(barrier, 4)
 
     def remote(src, dst, send, recv, who):
         return pltpu.make_async_remote_copy(
@@ -230,23 +225,19 @@
 
     peers = []
     edges = []
+    relays = []
     for m in range(members):
         peers.append(remote(st_hbm.at[m], peer.at[m], peer_send.at[m], peer_recv.at[m], (band, mate)))
         edges.append(
-            [
-                remote(
-                    st_hbm.at[m, lat_dev - 1],
-                    edge.at[s, m],
-                    edge_send.at[s, m],
-                    edge_recv.at[s, m],
-                    (next_band, who),
-                )
-                for s, who in enumerate((az, mate))
-            ]
+            remote(
+                st_hbm.at[m, lat_dev - 1], edge.at[0, m], edge_send.at[m], edge_recv.at[m], (next_band, az)
+            )
+        )
+        relays.append(
+            remote(edge.at[0, m], edge.at[1, m], relay_send.at[m], relay_recv.at[m], (band, mate))
         )
     for m in range(members):
-        for copy in edges[m]:
-            copy.start()
+        edges[m].start()
         peers[m].start()
     load_in.start()
     load_out.start()
@@ -323,15 +314,16 @@
     mine = 2 * core
     theirs = 2 - 2 * core
     for m in range(members):
+        edges[m].wait()
+        relays[m].start()
         loads[m].wait()
         for lat in range(lat_dev):
             unpack(st.at[m, lat], m, lat + 1, mine)
+        unpack(edge.at[0, m], m, 0, mine)
         peers[m].wait()
         for lat in range(lat_dev):
             unpack(peer.at[m, lat], m, lat + 1, theirs)
-        for copy in edges[m]:
-            copy.wait()
-        unpack(edge.at[0, m], m, 0, mine)
+        relays[m].wait()
         unpack(edge.at[1, m], m, 0, theirs)
         correlate_member(m)
         for j in range(2):
@@ -383,12 +375,6 @@
         + [jnp.zeros((WIDE - at - 3 * extra, embed), jnp.float32)],
         axis=0,
     ).astype(jnp.bfloat16)
-    stores = [
-        pltpu.make_async_copy(src, dst, store_sem.at[i])
-        for i, (src, dst) in enumerate(((first, first_out), (rest, rest_out), (second, second_out)))
-    ]
-    for copy in stores:
-        copy.start()
 
     count = lon_dev // 2
     room = rows_f32.shape[1]
@@ -420,51 +406,40 @@
             jnp.bfloat16
         )
 
-    def early_piece(k, carry):
+    def store_of(k):
+        return pltpu.make_async_copy(result, early_out.at[k], result_sem)
+
+    def piece(k, carry):
         left[...] = finish_part(k)
         total = mlp_rows(fields, extra, left[...], first, rest, second, held)()
+
+        @pl.when(k > 0)
+        def _():
+            store_of(k - 1).wait()
+
         result[...] = total[: count * GROUP].reshape(count, GROUP, embed)
-        copy = pltpu.make_async_copy(result, early_out.at[k], result_sem)
+        store_of(k).start()
+        return carry
+
+    lax.fori_loop(0, pieces, piece, 0)
+    store_of(pieces - 1).wait()
+
+
+def deliver(made, out, passing, in_sem, out_sem):
+    pieces, count = made.shape[:2]
+    inward = [pltpu.make_async_copy(made.at[k], passing.at[k], in_sem.at[k]) for k in range(pieces)]
+    outward = [
+        pltpu.make_async_copy(
+            passing.at[k], out.at[k // 2, pl.ds(k % 2 * count, count)], out_sem.at[k]
+        )
+        for k in range(pieces)
+    ]
+    for copy in inward:
         copy.start()
-        copy.wait()
-        return carry
-
-    if early:
-        lax.fori_loop(0, early, early_piece, 0)
-    for k in range(early, pieces):
-        left_out[k - early] = finish_part(k)
-    for copy in stores:
-        copy.wait()
-
-
-def mlp(
-    fields, extra, early, left_ref, first, rest, second_hbm, early_in, out, second, held, result, load_sem, move_sem, result_sem
-):
-    late = left_ref.shape[0]
-    count = result.shape[0]
-    embed = result.shape[2]
-    load = pltpu.make_async_copy(second_hbm, second, load_sem)
-    load.start()
-    moves = [
-        pltpu.make_async_copy(
-            early_in.at[k], out.at[k // 2, pl.ds(k % 2 * count, count)], move_sem.at[k]
-        )
-        for k in range(early)
-    ]
-    for copy in moves:
-        copy.start()
-    for i in range(late):
-        k = early + i
-        finish = mlp_rows(fields, extra, left_ref[i], first, rest, second, held)
-        if i == 0:
-            load.wait()
-        result[...] = finish()[: count * GROUP].reshape(count, GROUP, embed)
-        copy = pltpu.make_async_copy(
-            result, out.at[k // 2, pl.ds(k % 2 * count, count)], result_sem
-        )
-        copy.start()
-        copy.wait()
-    for copy in moves:
+    for come, go in zip(inward, outward):
+        come.wait()
+        go.start()
+    for copy in outward:
         copy.wait()
 
 
@@ -472,8 +447,6 @@
     members, lat_dev, fields, lon_dev = state.shape
     lat_half = lat_dev // 2
     pieces = 2 * members
-    early = min(EARLY, pieces - 1)
-    late = pieces - early
     count = lon_dev // 2
     embed, ffn = w_in.shape
     main = ffn // WIDE * WIDE
@@ -485,17 +458,11 @@
     half = jnp.bfloat16
     dma = pltpu.SemaphoreType.DMA
     packed = (pieces, GROUP - 1, fields, LANES)
-    left, first, rest, second, ready = pl.pallas_call(
-        functools.partial(exchange, bands, columns, early),
-        out_shape=(
-            jax.ShapeDtypeStruct((late, room, WIDE), half),
-            jax.ShapeDtypeStruct((WIDE, main), half),
-            jax.ShapeDtypeStruct((WIDE, WIDE), half),
-            jax.ShapeDtypeStruct((depth, embed), half),
-            jax.ShapeDtypeStruct((early, count, GROUP, embed), f32),
-        ),
+    made = pl.pallas_call(
+        functools.partial(exchange, bands, columns),
+        out_shape=jax.ShapeDtypeStruct((pieces, count, GROUP, embed), f32),
         in_specs=[pl.BlockSpec(memory_space=pltpu.SMEM)] + [vmem] * 3 + [hbm] * 3,
-        out_specs=(vmem,) + (hbm,) * 4,
+        out_specs=hbm,
         scratch_shapes=[
             pltpu.VMEM(state.shape, f32),
             pltpu.VMEM(w_in.shape, f32),
@@ -515,12 +482,13 @@
             pltpu.VMEM((2,) + packed, f32),
             pltpu.VMEM((2,) + packed, f32),
             dma((members + 2,)),
-            dma((3,)),
             dma(()),
             dma((members,)),
             dma((members,)),
-            dma((2, members)),
-            dma((2, members)),
+            dma((members,)),
+            dma((members,)),
+            dma((members,)),
+            dma((members,)),
             dma((2, pieces)),
             dma((2, pieces)),
         ],
@@ -538,21 +506,18 @@
         w_out.T,
     )
     out = pl.pallas_call(
-        functools.partial(mlp, fields, ffn - main, early),
+        deliver,
         out_shape=jax.ShapeDtypeStruct((members, lon_dev, lat_half, embed), f32),
-        in_specs=[vmem] * 3 + [hbm] * 2,
+        in_specs=[hbm],
         out_specs=hbm,
         scratch_shapes=[
-            pltpu.VMEM((depth, embed), half),
-            pltpu.VMEM((room, depth), half),
-            pltpu.VMEM((count, GROUP, embed), f32),
-            dma(()),
-            dma((early,)),
-            dma(()),
+            pltpu.VMEM((pieces, count, GROUP, embed), f32),
+            dma((pieces,)),
+            dma((pieces,)),
         ],
-        compiler_params=pltpu.CompilerParams(vmem_limit_bytes=56 * 2**20),
-        name="mlp",
-    )(left, first, rest, second, ready)
+        compiler_params=pltpu.CompilerParams(vmem_limit_bytes=32 * 2**20),
+        name="deliver",
+    )(made)
     return jnp.transpose(out, (0, 2, 1, 3))
 
 

time: 138 us -> 43.3 us (0.31)
  Pallas kernels: 137 us -> 40.9 us
  local copies, waits for them, and re-layouts: 0 us -> 2.25 us
    pallas_call x2, Pallas kernels: 137 us -> 40.9 us  [the longest x1 38.1 us: per_device_fast(): pl.pallas_call(functools.partial(exchange, bands, columns), out_shape=jax...]
    unnamed x0 -> x2, local copies, waits for them, and re-layouts: none -> 2.25 us
where the time goes in v1:
time: 43.3 us; the launch traced here: 43.1 us
  Pallas kernels  40.9 us (94%)
  local copies, waits for them, and re-layouts  2.25 us (5%)
    pallas_call x1, Pallas kernels, per_device_fast(): pl.pallas_call(functools.partial(exchange, bands, columns), out_shape=jax...  38.1 us
    pallas_call x1, Pallas kernels, per_device_fast(): pl.pallas_call(deliver, out_shape=jax.ShapeDtypeStruct((members, lon_dev,...  2.73 us
    unnamed x2, local copies, waits for them, and re-layouts  2.25 us

profile of v1, /device:TPU:0, one launch (start us, length us, event | category | flops | bytes accessed | tf_op | source)
XLA Modules:
  0.0 43.1 jit_solution(2410973128738913569)
XLA Ops:
  0.0 38.1 %exchange.1.made = f32[4,90,4,641]{3,2,1,0:T(4,128)} custom-call(s32[16]{0:T(128)} %idx_ref.1, f32[9,9,3,72]{3,2,1,0:T(4,128)} %bitcast.4, f32[72,641]{1,0:T(8,128)} %w_mix.1, f32[1282]{0:T(1024)} %b_in.1, f32[2,8,72,180]{3,2,1,0:T(8,128)} %st_hbm.1, f32[641,1282]{1,0:T(8,128)} %w_in_hbm.1, f32[641,1282]{1,0:T(8,128)} %bitcast.3), custom_call_target="tpu_custom_call" | custom-call | tf_op jit(solution)/shard_map/exchange/pallas_call | solution.py:461
  38.2 0.0 copy-start
  38.2 2.2 %copy-done = f32[4,90,4,641]{3,2,1,0:T(4,128)S(1)} copy-done((f32[4,90,4,641]{3,2,1,0:T(4,128)S(1)}, f32[4,90,4,641]{3,2,1,0:T(4,128)}, u32[]{:S(2)}) %copy-start) | copy-done | bytes 3692184
  40.4 2.7 %deliver.1 = f32[2,180,4,641]{3,2,1,0:T(4,128)} custom-call(f32[4,90,4,641]{3,2,1,0:T(4,128)S(1)} %copy-done), custom_call_target="tpu_custom_call" | custom-call | tf_op jit(solution)/shard_map/deliver/pallas_call | solution.py:508
Async XLA Ops:
  38.2 2.3 %copy-start = (f32[4,90,4,641]{3,2,1,0:T(4,128)S(1)}, f32[4,90,4,641]{3,2,1,0:T(4,128)}, u32[]{:S(2)}) copy-start(f32[4,90,4,641]{3,2,1,0:T(4,128)} %exchange.1.made) | copy-start | bytes 11076484

commit v2 on v1

--- a/solution.py
+++ b/solution.py
@@ -1,4 +1,5 @@
 import functools
+import math
 
 import jax
 import jax.numpy as jnp
@@ -125,31 +126,55 @@
     return -(-(lon_dev // 2 * GROUP) // 16) * 16
 
 
+ERFC = (0.254829592, -0.284496736, 1.421413741, -1.453152027, 1.061405429)
+ERFC_P = 0.3275911
+
+
+def gelu(x):
+    size = jnp.abs(x)
+    base = size * (ERFC_P * 0.5**0.5) + 1.0
+    guess = pl.reciprocal(base, approx=True)
+    t = guess * (2.0 - base * guess)
+    poly = ERFC[4] * 0.5
+    for coefficient in ERFC[3::-1]:
+        poly = poly * t + coefficient * 0.5
+    upper = poly * t * jnp.exp2(x * x * (-0.5 / math.log(2.0)))
+    return jnp.maximum(x, 0.0) - size * upper
+
+
 def mlp_rows(fields, extra, left16, first, rest, second, held):
-    main = first.shape[1]
+    chunks = first.shape[1] // WIDE
     at = 3 * fields + 3
     low_at = at + 2 * extra
 
     def act(weights):
-        pre = jnp.dot(left16, weights, preferred_element_type=jnp.float32)
-        return pre * 0.5 * (1.0 + lax.erf(pre * (0.5**0.5)))
-
-    for c in range(main // WIDE):
+        return gelu(jnp.dot(left16, weights, preferred_element_type=jnp.float32))
+
+    total = None
+    done = 0
+    for c in range(chunks):
         hidden = act(first[:, c * WIDE : (c + 1) * WIDE])
         top = hidden.astype(jnp.bfloat16)
         low = (hidden - top.astype(jnp.float32)).astype(jnp.bfloat16)
-        held[:, c * WIDE : (c + 1) * WIDE] = top
-        held[:, main + c * WIDE : main + (c + 1) * WIDE] = top
-        held[:, 2 * main + c * WIDE : 2 * main + (c + 1) * WIDE] = low
-    top, low = halves(act(rest[...]))
-    lane = lax.broadcasted_iota(jnp.int32, top.shape, 1)
-    mixed = jnp.where(
-        lane < at,
-        left16.astype(jnp.float32),
-        jnp.where(lane < low_at, top, jnp.where(lane < low_at + extra, low, 0.0)),
-    )
-    held[:, 3 * main :] = mixed.astype(jnp.bfloat16)
-    return lambda: jnp.dot(held[...], second[...], preferred_element_type=jnp.float32)
+        base = 3 * c * WIDE
+        held[:, base : base + WIDE] = top
+        held[:, base + WIDE : base + 2 * WIDE] = top
+        held[:, base + 2 * WIDE : base + 3 * WIDE] = low
+        if c == chunks - 1:
+            top, low = halves(act(rest[...]))
+            lane = lax.broadcasted_iota(jnp.int32, top.shape, 1)
+            mixed = jnp.where(
+                lane < at,
+                left16.astype(jnp.float32),
+                jnp.where(lane < low_at, top, jnp.where(lane < low_at + extra, low, 0.0)),
+            )
+            held[:, 3 * chunks * WIDE :] = mixed.astype(jnp.bfloat16)
+        if c % 2 == 1 or c == chunks - 1:
+            upto = base + 3 * WIDE if c < chunks - 1 else held.shape[1]
+            term = jnp.dot(held[:, done:upto], second[done:upto, :], preferred_element_type=jnp.float32)
+            total = term if total is None else total + term
+            done = upto
+    return total
 
 
 def exchange(
@@ -280,7 +305,7 @@
             rows = pl.ds(pl.multiple_of(r * SUB, SUB), SUB)
             total = [[[None] * lat_half for _ in range(2)] for _ in range(3)]
             for o in range(lat_half):
-                for a in range(3):
+                for a in range(1 if o == 0 else 0, 3):
                     x = [blocks[m, 2 * o + a, b, rows, :] for b in range(4)]
                     for target in range(3):
                         base = pad + half * target - 2 * core
@@ -299,6 +324,25 @@
 
         lax.fori_loop(0, tiles, body, 0)
 
+    def add_edge(m):
+        def body(r, carry):
+            rows = pl.ds(pl.multiple_of(r * SUB, SUB), SUB)
+            lane = lax.broadcasted_iota(jnp.int32, (SUB, LANES), 1)
+            x = [blocks[m, 0, b, rows, :] for b in range(4)]
+            for target in range(3):
+                base = pad + half * target - 2 * core
+                w = {d: taps[0, base + d, rows, :] for d in range(-1, 4)}
+                for j in range(2):
+                    term = w[-j] * x[0]
+                    for b in range(1, 4):
+                        term = term + w[b - j] * x[b]
+                    ref = own if target == 1 else outgoing.at[target // 2]
+                    old = ref[2 * m + j, 0, rows, :]
+                    ref[2 * m + j, 0, rows, :] = old + jnp.where(lane < SPACING, term, 0.0)
+            return carry
+
+        lax.fori_loop(0, tiles, body, 0)
+
     def parts(k):
         return [
             remote(
@@ -314,21 +358,26 @@
     mine = 2 * core
     theirs = 2 - 2 * core
     for m in range(members):
-        edges[m].wait()
-        relays[m].start()
         loads[m].wait()
         for lat in range(lat_dev):
             unpack(st.at[m, lat], m, lat + 1, mine)
-        unpack(edge.at[0, m], m, 0, mine)
+        if m == 0:
+            edges[0].wait()
+            relays[0].start()
         peers[m].wait()
         for lat in range(lat_dev):
             unpack(peer.at[m, lat], m, lat + 1, theirs)
+        correlate_member(m)
+        unpack(edge.at[0, m], m, 0, mine)
         relays[m].wait()
         unpack(edge.at[1, m], m, 0, theirs)
-        correlate_member(m)
+        add_edge(m)
         for j in range(2):
             for copy in parts(2 * m + j):
                 copy.start()
+        if m + 1 < members:
+            edges[m + 1].wait()
+            relays[m + 1].start()
 
     main = ffn // WIDE * WIDE
     extra = ffn - main
@@ -365,10 +414,10 @@
     load_out.wait()
     for c in range(main // WIDE):
         top, low = halves(w_out[:, c * WIDE : (c + 1) * WIDE].T)
-        base = c * WIDE
+        base = 3 * c * WIDE
         second[base : base + WIDE, :] = top.astype(jnp.bfloat16)
-        second[base + main : base + main + WIDE, :] = low.astype(jnp.bfloat16)
-        second[base + 2 * main : base + 2 * main + WIDE, :] = top.astype(jnp.bfloat16)
+        second[base + WIDE : base + 2 * WIDE, :] = low.astype(jnp.bfloat16)
+        second[base + 2 * WIDE : base + 3 * WIDE, :] = top.astype(jnp.bfloat16)
     top, low = halves(w_out[:, main:].T)
     second[3 * main :, :] = jnp.concatenate(
         [mix_top, mix_low, mix_top, jnp.zeros((3, embed), jnp.float32), top, low, top]
@@ -411,7 +460,7 @@
 
     def piece(k, carry):
         left[...] = finish_part(k)
-        total = mlp_rows(fields, extra, left[...], first, rest, second, held)()
+        total = mlp_rows(fields, extra, left[...], first, rest, second, held)
 
         @pl.when(k > 0)
         def _():
@@ -515,7 +564,7 @@
             dma((pieces,)),
             dma((pieces,)),
         ],
-        compiler_params=pltpu.CompilerParams(vmem_limit_bytes=32 * 2**20),
+        compiler_params=pltpu.CompilerParams(vmem_limit_bytes=60 * 2**20),
         name="deliver",
     )(made)
     return jnp.transpose(out, (0, 2, 1, 3))

time: 43.3 us -> 42.7 us (0.986)
  local copies, waits for them, and re-layouts: 2.25 us -> 0 us
  Pallas kernels: 40.9 us -> 42.6 us
    unnamed x2 -> x0, local copies, waits for them, and re-layouts: 2.25 us -> none
    pallas_call x1, Pallas kernels: 38.1 us -> 39.1 us  [per_device_fast(): pl.pallas_call(functools.partial(exchange, bands, columns), out_shape=jax...]
    pallas_call x1, Pallas kernels: 2.73 us -> 3.47 us  [per_device_fast(): pl.pallas_call(deliver, out_shape=jax.ShapeDtypeStruct((members, lon_dev,...]
where the time goes in v2:
time: 42.7 us; the launch traced here: 42.6 us
  Pallas kernels  42.6 us (100%)
    pallas_call x1, Pallas kernels, per_device_fast(): pl.pallas_call(functools.partial(exchange, bands, columns), out_shape=jax...  39.1 us
    pallas_call x1, Pallas kernels, per_device_fast(): pl.pallas_call(deliver, out_shape=jax.ShapeDtypeStruct((members, lon_dev,...  3.47 us

profile of v2, /device:TPU:0, one launch (start us, length us, event | category | flops | bytes accessed | tf_op | source)
XLA Modules:
  0.0 42.6 jit_solution(10119362956169977989)
XLA Ops:
  0.0 39.1 %exchange.1.made = f32[4,90,4,641]{3,2,1,0:T(4,128)} custom-call(s32[16]{0:T(128)} %idx_ref.1, f32[9,9,3,72]{3,2,1,0:T(4,128)} %bitcast.4, f32[72,641]{1,0:T(8,128)} %w_mix.1, f32[1282]{0:T(1024)} %b_in.1, f32[2,8,72,180]{3,2,1,0:T(8,128)} %st_hbm.1, f32[641,1282]{1,0:T(8,128)} %w_in_hbm.1, f32[641,1282]{1,0:T(8,128)} %bitcast.3), custom_call_target="tpu_custom_call" | custom-call | tf_op jit(solution)/shard_map/exchange/pallas_call | solution.py:510
  39.1 3.5 %deliver.1 = f32[2,180,4,641]{3,2,1,0:T(4,128)} custom-call(f32[4,90,4,641]{3,2,1,0:T(4,128)} %exchange.1.made), custom_call_target="tpu_custom_call" | custom-call | tf_op jit(solution)/shard_map/deliver/pallas_call | solution.py:557

commit v3 on v2

--- a/solution.py
+++ b/solution.py
@@ -227,8 +227,8 @@
     chip = az // 2
     chips = columns // 2
     mate = chip * 2 + 1 - core
-    up = lax.rem(chip + 1, chips) * 2 + core
-    down = lax.rem(chip + chips - 1, chips) * 2 + core
+    near = lax.rem(chip + chips - 1 + 2 * core, chips) * 2 + core
+    far = lax.rem(chip + chips + 1 - 2 * core, chips) * 2 + core
     next_band = lax.rem(band + 1, bands)
     last_band = lax.rem(band + bands - 1, bands)
 
@@ -239,7 +239,7 @@
         copy.start()
 
     barrier = pltpu.get_barrier_semaphore()
-    for who in ((band, mate), (band, up), (band, down), (last_band, az)):
+    for who in ((band, mate), (band, near), (band, far), (last_band, az)):
         pl.semaphore_signal(barrier, inc=1, device_id=who, device_id_type=MESH)
     pl.semaphore_wait(barrier, 4)
 
@@ -300,84 +300,87 @@
         ref[at + (1, rows, slice(None))] = jnp.where(lane < turns[2], turned[1], turned[2])
         ref[at + (2, rows, slice(None))] = jnp.where(lane < turns[3], turned[2], turned[3])
 
-    def correlate_member(m):
+    mine = 2 * core
+    theirs = 2 - 2 * core
+    plans = {
+        "near": (2, mine, pad + 2 * half * (1 - core), lambda k: outgoing.at[0, k]),
+        "far": (4, 0, pad + 2 * (half - 1) * core, lambda k: outgoing.at[1, k]),
+        "own": (4, 0, pad + half - 2 * core, lambda k: own.at[k]),
+    }
+
+    def terms(x, tap, base, rows):
+        w = {d: taps[tap, base + d, rows, :] for d in range(-1, len(x))}
+        sums = []
+        for j in range(2):
+            term = w[-j] * x[0]
+            for b in range(1, len(x)):
+                term = term + w[b - j] * x[b]
+            sums.append(term)
+        return sums
+
+    def correlate_part(m, plan, with_edge):
+        width, start, base, ref_of = plans[plan]
+
         def body(r, carry):
             rows = pl.ds(pl.multiple_of(r * SUB, SUB), SUB)
-            total = [[[None] * lat_half for _ in range(2)] for _ in range(3)]
+            total = [[None] * lat_half for _ in range(2)]
             for o in range(lat_half):
-                for a in range(1 if o == 0 else 0, 3):
-                    x = [blocks[m, 2 * o + a, b, rows, :] for b in range(4)]
-                    for target in range(3):
-                        base = pad + half * target - 2 * core
-                        w = {d: taps[o * 3 + a, base + d, rows, :] for d in range(-1, 4)}
-                        for j in range(2):
-                            term = w[-j] * x[0]
-                            for b in range(1, 4):
-                                term = term + w[b - j] * x[b]
-                            old = total[target][j][o]
-                            total[target][j][o] = term if old is None else old + term
+                for a in range(1 if o == 0 and not with_edge else 0, 3):
+                    x = [blocks[m, 2 * o + a, start + b, rows, :] for b in range(width)]
+                    for j, term in enumerate(terms(x, o * 3 + a, base, rows)):
+                        old = total[j][o]
+                        total[j][o] = term if old is None else old + term
             for j in range(2):
-                pack(total[0][j], outgoing, (0, 2 * m + j), rows)
-                pack(total[1][j], own, (2 * m + j,), rows)
-                pack(total[2][j], outgoing, (1, 2 * m + j), rows)
+                pack(total[j], ref_of(2 * m + j), (), rows)
             return carry
 
         lax.fori_loop(0, tiles, body, 0)
 
-    def add_edge(m):
+    def add_edge(m, plan):
+        width, start, base, ref_of = plans[plan]
+
         def body(r, carry):
             rows = pl.ds(pl.multiple_of(r * SUB, SUB), SUB)
             lane = lax.broadcasted_iota(jnp.int32, (SUB, LANES), 1)
-            x = [blocks[m, 0, b, rows, :] for b in range(4)]
-            for target in range(3):
-                base = pad + half * target - 2 * core
-                w = {d: taps[0, base + d, rows, :] for d in range(-1, 4)}
-                for j in range(2):
-                    term = w[-j] * x[0]
-                    for b in range(1, 4):
-                        term = term + w[b - j] * x[b]
-                    ref = own if target == 1 else outgoing.at[target // 2]
-                    old = ref[2 * m + j, 0, rows, :]
-                    ref[2 * m + j, 0, rows, :] = old + jnp.where(lane < SPACING, term, 0.0)
+            x = [blocks[m, 0, start + b, rows, :] for b in range(width)]
+            for j, term in enumerate(terms(x, 0, base, rows)):
+                ref = ref_of(2 * m + j)
+                ref[0, rows, :] = ref[0, rows, :] + jnp.where(lane < SPACING, term, 0.0)
             return carry
 
         lax.fori_loop(0, tiles, body, 0)
 
-    def parts(k):
-        return [
-            remote(
-                outgoing.at[way, k],
-                incoming.at[way, k],
-                part_send.at[way, k],
-                part_recv.at[way, k],
-                (band, who),
-            )
-            for way, who in enumerate((up, down))
-        ]
-
-    mine = 2 * core
-    theirs = 2 - 2 * core
+    def part(way, k):
+        return remote(
+            outgoing.at[way, k],
+            incoming.at[way, k],
+            part_send.at[way, k],
+            part_recv.at[way, k],
+            (band, (near, far)[way]),
+        )
+
     for m in range(members):
         loads[m].wait()
         for lat in range(lat_dev):
             unpack(st.at[m, lat], m, lat + 1, mine)
-        if m == 0:
-            edges[0].wait()
-            relays[0].start()
+        correlate_part(m, "near", False)
+        edges[m].wait()
+        relays[m].start()
+        unpack(edge.at[0, m], m, 0, mine)
+        add_edge(m, "near")
+        for j in range(2):
+            part(0, 2 * m + j).start()
         peers[m].wait()
         for lat in range(lat_dev):
             unpack(peer.at[m, lat], m, lat + 1, theirs)
-        correlate_member(m)
-        unpack(edge.at[0, m], m, 0, mine)
+        correlate_part(m, "far", False)
         relays[m].wait()
         unpack(edge.at[1, m], m, 0, theirs)
-        add_edge(m)
+        add_edge(m, "far")
         for j in range(2):
-            for copy in parts(2 * m + j):
-                copy.start()
-        if m + 1 < members:
-            edges[m + 1].wait()
-            relays[m + 1].start()
+            part(1, 2 * m + j).start()
+    for m in range(members):
+        correlate_part(m, "own", True)
 
     main = ffn // WIDE * WIDE
     extra = ffn - main
@@ -431,8 +434,8 @@
         rows_f32[side, count * GROUP :, :] = jnp.zeros((room - count * GROUP, LANES), jnp.float32)
 
     def finish_part(k):
-        for copy in parts(k):
-            copy.wait()
+        for way in range(2):
+            part(way, k).wait()
         v = [own[k, i] + incoming[0, k, i] + incoming[1, k, i] for i in range(GROUP - 1)]
         lane = lax.broadcasted_iota(jnp.int32, v[0].shape, 1)
         fields_of = [v[0]]
@@ -474,15 +477,23 @@
     store_of(pieces - 1).wait()
 
 
-def deliver(made, out, passing, in_sem, out_sem):
+def deliver(cuts, made, out, passing, in_sem, out_sem):
     pieces, count = made.shape[:2]
-    inward = [pltpu.make_async_copy(made.at[k], passing.at[k], in_sem.at[k]) for k in range(pieces)]
-    outward = [
-        pltpu.make_async_copy(
-            passing.at[k], out.at[k // 2, pl.ds(k % 2 * count, count)], out_sem.at[k]
-        )
-        for k in range(pieces)
-    ]
+    step = count // cuts
+    inward = []
+    outward = []
+    for k in range(pieces):
+        for c in range(cuts):
+            rows = pl.ds(c * step, step)
+            i = k * cuts + c
+            inward.append(pltpu.make_async_copy(made.at[k, rows], passing.at[k, rows], in_sem.at[i]))
+            outward.append(
+                pltpu.make_async_copy(
+                    passing.at[k, rows],
+                    out.at[k // 2, pl.ds(k % 2 * count + c * step, step)],
+                    out_sem.at[i],
+                )
+            )
     for copy in inward:
         copy.start()
     for come, go in zip(inward, outward):
@@ -554,15 +565,16 @@
         w_in,
         w_out.T,
     )
+    cuts = 3 if count % 3 == 0 else 1
     out = pl.pallas_call(
-        deliver,
+        functools.partial(deliver, cuts),
         out_shape=jax.ShapeDtypeStruct((members, lon_dev, lat_half, embed), f32),
         in_specs=[hbm],
         out_specs=hbm,
         scratch_shapes=[
             pltpu.VMEM((pieces, count, GROUP, embed), f32),
-            dma((pieces,)),
-            dma((pieces,)),
+            dma((pieces * cuts,)),
+            dma((pieces * cuts,)),
         ],
         compiler_params=pltpu.CompilerParams(vmem_limit_bytes=60 * 2**20),
         name="deliver",

time: 42.7 us -> 43.9 us (1.028)
  Pallas kernels: 42.6 us -> 43.8 us
    pallas_call x1, Pallas kernels: 39.1 us -> 39.8 us  [per_device_fast(): pl.pallas_call(functools.partial(exchange, bands, columns), out_shape=jax...]
    pallas_call x1, Pallas kernels: 3.47 us -> 3.96 us  [per_device_fast(): pl.pallas_call(functools.partial(deliver, cuts), out_shape=jax.ShapeDtype...]
where the time goes in v3:
time: 43.9 us; the launch traced here: 43.8 us
  Pallas kernels  43.8 us (100%)
    pallas_call x1, Pallas kernels, per_device_fast(): pl.pallas_call(functools.partial(exchange, bands, columns), out_shape=jax...  39.8 us
    pallas_call x1, Pallas kernels, per_device_fast(): pl.pallas_call(functools.partial(deliver, cuts), out_shape=jax.ShapeDtype...  3.96 us

profile of v3, /device:TPU:0, one launch (start us, length us, event | category | flops | bytes accessed | tf_op | source)
XLA Modules:
  0.0 43.8 jit_solution(11974011792733016887)
XLA Ops:
  0.0 39.8 %exchange.1.made = f32[4,90,4,641]{3,2,1,0:T(4,128)} custom-call(s32[16]{0:T(128)} %idx_ref.1, f32[9,9,3,72]{3,2,1,0:T(4,128)} %bitcast.4, f32[72,641]{1,0:T(8,128)} %w_mix.1, f32[1282]{0:T(1024)} %b_in.1, f32[2,8,72,180]{3,2,1,0:T(8,128)} %st_hbm.1, f32[641,1282]{1,0:T(8,128)} %w_in_hbm.1, f32[641,1282]{1,0:T(8,128)} %bitcast.3), custom_call_target="tpu_custom_call" | custom-call | tf_op jit(solution)/shard_map/exchange/pallas_call | solution.py:521
  39.8 4.0 %deliver.1 = f32[2,180,4,641]{3,2,1,0:T(4,128)} custom-call(f32[4,90,4,641]{3,2,1,0:T(4,128)} %exchange.1.made), custom_call_target="tpu_custom_call" | custom-call | tf_op jit(solution)/shard_map/deliver/pallas_call | solution.py:569

commit v4 on v3

--- a/solution.py
+++ b/solution.py
@@ -368,8 +368,9 @@
         relays[m].start()
         unpack(edge.at[0, m], m, 0, mine)
         add_edge(m, "near")
-        for j in range(2):
-            part(0, 2 * m + j).start()
+        if m == 0:
+            for j in range(2):
+                part(0, j).start()
         peers[m].wait()
         for lat in range(lat_dev):
             unpack(peer.at[m, lat], m, lat + 1, theirs)
@@ -377,10 +378,17 @@
         relays[m].wait()
         unpack(edge.at[1, m], m, 0, theirs)
         add_edge(m, "far")
-        for j in range(2):
-            part(1, 2 * m + j).start()
+        if m == 0:
+            for j in range(2):
+                part(1, j).start()
     for m in range(members):
         correlate_part(m, "own", True)
+
+    def follow(k):
+        for way in range(2):
+            part(way, k - 2).wait_send()
+        for way in range(2):
+            part(way, k).start()
 
     main = ffn // WIDE * WIDE
     extra = ffn - main
@@ -414,6 +422,7 @@
         + [jnp.zeros((WIDE, WIDE - at - 3 * extra), jnp.float32)],
         axis=1,
     ).astype(jnp.bfloat16)
+    follow(2)
     load_out.wait()
     for c in range(main // WIDE):
         top, low = halves(w_out[:, c * WIDE : (c + 1) * WIDE].T)
@@ -428,6 +437,8 @@
         axis=0,
     ).astype(jnp.bfloat16)
 
+    for k in range(3, pieces):
+        follow(k)
     count = lon_dev // 2
     room = rows_f32.shape[1]
     for side in range(WIDE // LANES):
@@ -435,7 +446,7 @@
 
     def finish_part(k):
         for way in range(2):
-            part(way, k).wait()
+            part(way, k).wait_recv()
         v = [own[k, i] + incoming[0, k, i] + incoming[1, k, i] for i in range(GROUP - 1)]
         lane = lax.broadcasted_iota(jnp.int32, v[0].shape, 1)
         fields_of = [v[0]]
@@ -474,6 +485,9 @@
         return carry
 
     lax.fori_loop(0, pieces, piece, 0)
+    for k in range(pieces - 2, pieces):
+        for way in range(2):
+            part(way, k).wait_send()
     store_of(pieces - 1).wait()
 
 
@@ -565,7 +579,7 @@
         w_in,
         w_out.T,
     )
-    cuts = 3 if count % 3 == 0 else 1
+    cuts = 1
     out = pl.pallas_call(
         functools.partial(deliver, cuts),
         out_shape=jax.ShapeDtypeStruct((members, lon_dev, lat_half, embed), f32),

time: 43.9 us -> 43.4 us (0.989)
  Pallas kernels: 43.8 us -> 43.2 us
    pallas_call x1, Pallas kernels: 3.96 us -> 3.47 us  [per_device_fast(): pl.pallas_call(functools.partial(deliver, cuts), out_shape=jax.ShapeDtype...]
where the time goes in v4:
time: 43.4 us; the launch traced here: 43.3 us
  Pallas kernels  43.2 us (100%)
    pallas_call x1, Pallas kernels, per_device_fast(): pl.pallas_call(functools.partial(exchange, bands, columns), out_shape=jax...  39.8 us
    pallas_call x1, Pallas kernels, per_device_fast(): pl.pallas_call(functools.partial(deliver, cuts), out_shape=jax.ShapeDtype...  3.47 us

profile of v4, /device:TPU:0, one launch (start us, length us, event | category | flops | bytes accessed | tf_op | source)
XLA Modules:
  0.0 43.3 jit_solution(14173631100177178133)
XLA Ops:
  0.0 39.8 %exchange.1.made = f32[4,90,4,641]{3,2,1,0:T(4,128)} custom-call(s32[16]{0:T(128)} %idx_ref.1, f32[9,9,3,72]{3,2,1,0:T(4,128)} %bitcast.4, f32[72,641]{1,0:T(8,128)} %w_mix.1, f32[1282]{0:T(1024)} %b_in.1, f32[2,8,72,180]{3,2,1,0:T(8,128)} %st_hbm.1, f32[641,1282]{1,0:T(8,128)} %w_in_hbm.1, f32[641,1282]{1,0:T(8,128)} %bitcast.3), custom_call_target="tpu_custom_call" | custom-call | tf_op jit(solution)/shard_map/exchange/pallas_call | solution.py:535
  39.8 3.5 %deliver.1 = f32[2,180,4,641]{3,2,1,0:T(4,128)} custom-call(f32[4,90,4,641]{3,2,1,0:T(4,128)} %exchange.1.made), custom_call_target="tpu_custom_call" | custom-call | tf_op jit(solution)/shard_map/deliver/pallas_call | solution.py:583

commit v5 on v4

--- a/solution.py
+++ b/solution.py
@@ -241,29 +241,7 @@
     barrier = pltpu.get_barrier_semaphore()
     for who in ((band, mate), (band, near), (band, far), (last_band, az)):
         pl.semaphore_signal(barrier, inc=1, device_id=who, device_id_type=MESH)
-    pl.semaphore_wait(barrier, 4)
-
-    def remote(src, dst, send, recv, who):
-        return pltpu.make_async_remote_copy(
-            src_ref=src, dst_ref=dst, send_sem=send, recv_sem=recv, device_id=who, device_id_type=MESH
-        )
-
-    peers = []
-    edges = []
-    relays = []
-    for m in range(members):
-        peers.append(remote(st_hbm.at[m], peer.at[m], peer_send.at[m], peer_recv.at[m], (band, mate)))
-        edges.append(
-            remote(
-                st_hbm.at[m, lat_dev - 1], edge.at[0, m], edge_send.at[m], edge_recv.at[m], (next_band, az)
-            )
-        )
-        relays.append(
-            remote(edge.at[0, m], edge.at[1, m], relay_send.at[m], relay_recv.at[m], (band, mate))
-        )
-    for m in range(members):
-        edges[m].start()
-        peers[m].start()
+
     load_in.start()
     load_out.start()
 
@@ -280,6 +258,30 @@
             for t in range(pad):
                 taps[o * 3 + a, t] = jnp.zeros((fields, LANES), jnp.float32)
                 taps[o * 3 + a, t + pad + TAPS] = jnp.zeros((fields, LANES), jnp.float32)
+
+    pl.semaphore_wait(barrier, 4)
+
+    def remote(src, dst, send, recv, who):
+        return pltpu.make_async_remote_copy(
+            src_ref=src, dst_ref=dst, send_sem=send, recv_sem=recv, device_id=who, device_id_type=MESH
+        )
+
+    peers = []
+    edges = []
+    relays = []
+    for m in range(members):
+        peers.append(remote(st_hbm.at[m], peer.at[m], peer_send.at[m], peer_recv.at[m], (band, mate)))
+        edges.append(
+            remote(
+                st_hbm.at[m, lat_dev - 1], edge.at[0, m], edge_send.at[m], edge_recv.at[m], (next_band, az)
+            )
+        )
+        relays.append(
+            remote(edge.at[0, m], edge.at[1, m], relay_send.at[m], relay_recv.at[m], (band, mate))
+        )
+    for m in range(members):
+        edges[m].start()
+        peers[m].start()
 
     spare = lon_dev - LANES
 

time: 43.4 us -> 43.6 us (level)
  no operation moved by 1% of the time
where the time goes in v5:
time: 43.6 us; the launch traced here: 43.4 us
  Pallas kernels  43.4 us (100%)
    pallas_call x1, Pallas kernels, per_device_fast(): pl.pallas_call(functools.partial(exchange, bands, columns), out_shape=jax...  39.9 us
    pallas_call x1, Pallas kernels, per_device_fast(): pl.pallas_call(functools.partial(deliver, cuts), out_shape=jax.ShapeDtype...  3.47 us

profile of v5, /device:TPU:0, one launch (start us, length us, event | category | flops | bytes accessed | tf_op | source)
XLA Modules:
  0.0 43.4 jit_solution(13462371589780401617)
XLA Ops:
  0.0 39.9 %exchange.1.made = f32[4,90,4,641]{3,2,1,0:T(4,128)} custom-call(s32[16]{0:T(128)} %idx_ref.1, f32[9,9,3,72]{3,2,1,0:T(4,128)} %bitcast.4, f32[72,641]{1,0:T(8,128)} %w_mix.1, f32[1282]{0:T(1024)} %b_in.1, f32[2,8,72,180]{3,2,1,0:T(8,128)} %st_hbm.1, f32[641,1282]{1,0:T(8,128)} %w_in_hbm.1, f32[641,1282]{1,0:T(8,128)} %bitcast.3), custom_call_target="tpu_custom_call" | custom-call | tf_op jit(solution)/shard_map/exchange/pallas_call | solution.py:537
  39.9 3.5 %deliver.1 = f32[2,180,4,641]{3,2,1,0:T(4,128)} custom-call(f32[4,90,4,641]{3,2,1,0:T(4,128)} %exchange.1.made), custom_call_target="tpu_custom_call" | custom-call | tf_op jit(solution)/shard_map/deliver/pallas_call | solution.py:585
